TPU v7x, 32 devices: a whole 2x2x4 slice. The times are simulated.
32 devices in a mesh: grp: 2 (over y), lat: 4 (over z), lev: 2 (over x), fld: 2 (over core).
Axes of the slice: x: 2, y: 2, z: 4, core: 2. Of those that a mesh axis runs over, the one named last changes fastest.
Arguments:
- upstream: bfloat16 [16, 4, 1024, 2048], P('grp', 'fld', 'lat', 'lev'), parts along dimension 0, may hold values from -6 to 6
- departure: int32 [16, 1024, 2048], P('grp', 'lat', 'lev'), parts along dimension 0, may hold values from 0 to 3
- fractions: bfloat16 [2, 16, 1024, 2048], P(None, 'grp', 'lat', 'lev'), parts along dimension 1, may hold values from 0 to 1
- heating: bfloat16 [8, 1024, 2048], P(('grp', 'fld'), 'lat', 'lev'), parts along dimension 0, may hold values from -6 to 6
- mixing: float32 [4, 8, 8], P('fld'), may hold values from -2 to 2
- slot_wavenumber: int32 [8], replicated, may hold values from 0 to 7, as said below
- legendre: bfloat16 [8, 1024, 1024], P('lat', None, 'lev'), as said below
Outputs:
- spectrum: float32 [8, 1024, 4, 4, 8], P('lat', 'lev', 'grp', 'fld'), parts along dimension 2
There are 2 independent parts, one for each index of `grp`. A program takes and returns all parts, laid end to end along the dimension named above; an argument that names none is the same for every part. Nothing has to cross between parts.
Inputs may be any that keep to these rules, and one draw needn't show every extreme that they name: `slot_wavenumber`: each value appears exactly once. legendre[s, i, n] is the fully normalized associated Legendre function of degree n and order m_s at cos(theta_i), theta_i = (i + 0.5) pi / 1024, times sqrt(pi sin(theta_i) / 1024), zero for n < m_s, rounded to bfloat16.
All inputs are finite; a program needn't handle non-finite values.
Results may differ from a plain program's by a relative error of at most 0.0043.
Values may be sent and summed in bfloat16 or wider, within the bound.
A program may use at most 768 MiB of HBM per device.

v0:
```python
import math

import jax
import jax.numpy as jnp
from jax import lax
from jax.sharding import PartitionSpec as P

NLON = 2048
NTRUNC = 1024


def with_halo(shard, sides, width, wrap):
    for axis, dim in sides:
        peers, length = (lax.axis_size(axis), shard.shape[dim])
        up = [(i, (i + 1) % peers) for i in range(peers if wrap else peers - 1)]
        down = [(j, i) for i, j in up]
        last = lax.slice_in_dim(shard, length - width, length, axis=dim)
        leading = lax.slice_in_dim(shard, 0, width, axis=dim)
        before = lax.ppermute(last, axis, up)
        after = lax.ppermute(leading, axis, down)
        shard = jnp.concatenate([before, shard, after], axis=dim)
    return shard


def cubic_weights(fraction):
    return [
        -fraction * (fraction - 1.0) * (fraction - 2.0) / 6.0,
        (fraction + 1.0) * (fraction - 1.0) * (fraction - 2.0) / 2.0,
        -(fraction + 1.0) * fraction * (fraction - 2.0) / 2.0,
        (fraction + 1.0) * fraction * (fraction - 1.0) / 6.0,
    ]


def offset_weights(shift, weights):
    result = []
    for target in range(-2, 3):
        total = jnp.zeros(shift.shape, jnp.float32)
        for tap in range(4):
            total = total + jnp.where(shift + tap - 1 == target, weights[tap], 0.0)
        result.append(total)
    return jnp.stack(result)


def fourier_basis(first, count, waves):
    positions = first + jnp.arange(count, dtype=jnp.int32)
    phase = positions[:, None] * waves[None, :] % NLON
    angle = phase.astype(jnp.float32) * (2.0 * math.pi / NLON)
    return jnp.concatenate([jnp.cos(angle), -jnp.sin(angle)], axis=1).astype(jnp.bfloat16)


def shards(upstream, departure, fractions, heating, mixing, slot_wavenumber, legendre):
    levels, var_dev, lat_dev, lon_dev = upstream.shape
    widened = with_halo(upstream, (("lev", 3),), 2, True)
    padded = with_halo(widened, (("lat", 2),), 2, False)
    shift_lat = departure // 2 - 1
    shift_lon = departure % 2 - 1
    row_weights = offset_weights(shift_lat, cubic_weights(fractions[0].astype(jnp.float32)))
    col_weights = offset_weights(shift_lon, cubic_weights(fractions[1].astype(jnp.float32)))
    row_sums = []
    for row_off in range(5):
        windows = jnp.stack(
            [
                padded[:, :, row_off : row_off + lat_dev, col_off : col_off + lon_dev]
                for col_off in range(5)
            ]
        )
        row_sums.append(jnp.sum(windows.astype(jnp.float32) * col_weights[:, :, None], axis=0))
    interp = jnp.sum(jnp.stack(row_sums) * row_weights[:, :, None], axis=0)
    column = jnp.einsum("vlk,kvij->lvij", mixing, interp, precision=lax.Precision.HIGHEST)
    state = (interp + heating[None].astype(jnp.float32) * jnp.tanh(column)).astype(jnp.bfloat16)
    m_window = slot_wavenumber.shape[0]
    waves = slot_wavenumber * (NTRUNC // m_window)
    local_basis = fourier_basis(lax.axis_index("lev") * lon_dev, lon_dev, waves)
    sums = lax.psum_scatter(
        jnp.dot(
            state.reshape(-1, lon_dev), local_basis, preferred_element_type=jnp.float32
        ).reshape(
            levels // lax.axis_size("lev") * lax.axis_size("lev"), var_dev, lat_dev, 2 * m_window
        ),
        "lev",
        scatter_dimension=0,
        tiled=True,
    )
    coefficients = (
        (sums * (1.0 / math.sqrt(NLON)))
        .astype(jnp.bfloat16)
        .reshape(-1, var_dev, lat_dev, 2, m_window)
    )
    owned = lax.all_to_all(coefficients, "lat", split_axis=4, concat_axis=2, tiled=True)
    return jnp.einsum(
        "sin,lvirs->snrvl",
        legendre,
        lax.all_gather(owned, "lev", axis=0, tiled=True),
        preferred_element_type=jnp.float32,
    )


def solution(mesh):
    in_specs = (
        P("grp", "fld", "lat", "lev"),
        P("grp", "lat", "lev"),
        P(None, "grp", "lat", "lev"),
        P(("grp", "fld"), "lat", "lev"),
        P("fld", None, None),
        P(),
        P("lat", None, "lev"),
    )
    out_specs = P("lat", "lev", "grp", "fld", None)
    return jax.shard_map(shards, mesh=mesh, in_specs=in_specs, out_specs=out_specs, check_vma=False)
```

profile of v0, /device:TPU:0, one launch (start us, length us, event | category | flops | bytes accessed | tf_op | source)
XLA Modules:
  0.0 742.1 jit_solution(12218600054180028916)
XLA Ops:
  14.7 16.7 %bitcast_dynamic-update-slice_fusion.9 = f32[5,8,256,1024]{3,2,1,0:T(8,128)} fusion(bf16[2,8,256,1024]{3,2,1,0:T(8,128)(2,1)} %param.9, s32[8,256,1024]{2,1,0:T(8,128)} %param.8), kind=kLoop, calls=%fused_computation.152 | loop fusion | flops 98566144 | bytes 20971520
  31.4 27.7 %bitcast_dynamic-update-slice_fusion.8 = (f32[5,8,256,1024]{3,2,1,0:T(8,128)}, f32[5,8,256,1024]{3,2,1,0:T(8,128)}) fusion(f32[5,8,256,1024]{3,2,1,0:T(8,128)} %bitcast_dynamic-update-slice_fusion.9, bf16[2,8,256,1024]{3,2,1,0:T(8,128)(2,1)} %param.9, s32[8,256,1024]{2,1,0:T(8,128)} %param.8), kind=kLoop, calls=%fused_computation.151 | loop fusion | flops 174063616 | bytes 33554432
  59.1 25.9 %bitcast_dynamic-update-slice_fusion.7 = (f32[5,8,256,1024]{3,2,1,0:T(8,128)}, f32[5,8,256,1024]{3,2,1,0:T(8,128)}) fusion(f32[5,8,256,1024]{3,2,1,0:T(8,128)} %get-tuple-element.16, bf16[2,8,256,1024]{3,2,1,0:T(8,128)(2,1)S(1)} %bitcast.178, s32[8,256,1024]{2,1,0:T(8,128)S(1)} %bitcast.176, f32[5,8,256,1024]{3,2,1,0:T(8,128)} %get-tuple-element.17), kind=kLoop, calls=%fused_computation.150 | loop fusion | flops 174063616 | bytes 33554432
  85.0 26.4 %bitcast_dynamic-update-slice_fusion.6 = (f32[5,8,256,1024]{3,2,1,0:T(8,128)}, f32[5,8,256,1024]{3,2,1,0:T(8,128)}) fusion(f32[5,8,256,1024]{3,2,1,0:T(8,128)} %get-tuple-element.14, bf16[2,8,256,1024]{3,2,1,0:T(8,128)(2,1)S(1)} %bitcast.178, s32[8,256,1024]{2,1,0:T(8,128)S(1)} %bitcast.176, f32[5,8,256,1024]{3,2,1,0:T(8,128)} %get-tuple-element.15), kind=kLoop, calls=%fused_computation.149 | loop fusion | flops 174063616 | bytes 33554432
  111.4 13.0 %bitcast_dynamic-update-slice_fusion.12 = f32[5,8,256,1024]{3,2,1,0:T(8,128)} fusion(f32[5,8,256,1024]{3,2,1,0:T(8,128)} %get-tuple-element.13, bf16[2,8,256,1024]{3,2,1,0:T(8,128)(2,1)S(1)} %bitcast.178, s32[8,256,1024]{2,1,0:T(8,128)S(1)} %bitcast.176), kind=kLoop, calls=%fused_computation.155 | loop fusion | flops 90177536 | bytes 20971520
  124.4 27.5 %bitcast_dynamic-update-slice_fusion.5 = (f32[5,8,256,1024]{3,2,1,0:T(8,128)}, f32[5,8,256,1024]{3,2,1,0:T(8,128)}) fusion(f32[5,8,256,1024]{3,2,1,0:T(8,128)} %get-tuple-element.12, bf16[2,8,256,1024]{3,2,1,0:T(8,128)(2,1)} %param.9, s32[8,256,1024]{2,1,0:T(8,128)} %param.8, f32[5,8,256,1024]{3,2,1,0:T(8,128)} %bitcast_dynamic-update-slice_fusion.12), kind=kLoop, calls=%fused_computation.148 | loop fusion | flops 174063616 | bytes 33554432 | tf_op jit(solution)/shard_map/stack | solution.py:41
  164.6 17.4 %concatenate.40 = bf16[8,2,256,1028]{3,2,1,0:T(8,128)(2,1)} concatenate(bf16[8,2,256,2]{3,2,1,0:T(8,128)(2,1)S(1)} %copy.22, bf16[8,2,256,1024]{3,2,1,0:T(8,128)(2,1)} %param.7, bf16[8,2,256,2]{3,2,1,0:T(8,128)(2,1)} %copy.23), dimensions={3} | concatenate | bytes 16842752 | tf_op jit(solution)/shard_map/concatenate | solution.py:21
  188.7 11.6 %fusion.90 = bf16[5,8,2,256,1024]{4,3,2,1,0:T(8,128)(2,1)} fusion(bf16[5,8,2,256,1024]{4,3,2,1,0:T(8,128)(2,1)} %fusion.22, bf16[8,2,256,1024]{3,2,1,0:T(8,128)(2,1)} %param.7, bf16[8,2,256,2]{3,2,1,0:T(8,128)(2,1)S(1)} %copy.22), kind=kLoop, calls=%fused_computation.144 | loop fusion | flops 16777216 | bytes 16793600
  208.4 9.8 %fusion.19 = bf16[5,8,2,256,1024]{4,3,2,1,0:T(8,128)(2,1)} fusion(bf16[5,8,2,256,1024]{4,3,2,1,0:T(8,128)(2,1)} %bitcast_dynamic-update-slice_fusion.10, bf16[8,2,256,1024]{3,2,1,0:T(8,128)(2,1)} %param.7, bf16[8,2,256,2]{3,2,1,0:T(8,128)(2,1)S(1)} %copy-done.1), kind=kLoop, calls=%fused_computation.70 | loop fusion | flops 16777216 | bytes 16793600
  218.1 12.2 %fusion.88 = bf16[5,8,2,256,1024]{4,3,2,1,0:T(8,128)(2,1)} fusion(bf16[5,8,2,256,1024]{4,3,2,1,0:T(8,128)(2,1)} %fusion.19, bf16[8,2,256,2]{3,2,1,0:T(8,128)(2,1)S(1)} %copy-done.1, bf16[8,2,256,1024]{3,2,1,0:T(8,128)(2,1)} %param.7), kind=kLoop, calls=%fused_computation.141 | loop fusion | flops 16777216 | bytes 16793600 | tf_op jit(solution)/shard_map/stack | solution.py:61
  239.8 10.7 %fusion.81 = bf16[5,8,2,256,1024]{4,3,2,1,0:T(8,128)(2,1)} fusion(bf16[5,8,2,256,1024]{4,3,2,1,0:T(8,128)(2,1)} %fusion.78, bf16[8,2,2,1028]{3,2,1,0:T(2,128)(2,1)S(1)} %collective-permute-done.2, bf16[8,2,256,1028]{3,2,1,0:T(8,128)(2,1)} %concatenate.40), kind=kLoop, calls=%fused_computation.132 | loop fusion | flops 16777216 | bytes 17891584
  294.3 9.8 %fusion.86 = (bf16[5,8,2,256,1024]{4,3,2,1,0:T(8,128)(2,1)}, bf16[5,8,2,256,1024]{4,3,2,1,0:T(8,128)(2,1)}) fusion(bf16[5,8,2,256,1024]{4,3,2,1,0:T(8,128)(2,1)} %fusion.33, bf16[8,2,2,1028]{3,2,1,0:T(2,128)(2,1)S(1)} %collective-permute-done.3, bf16[8,2,256,1028]{3,2,1,0:T(8,128)(2,1)S(1)} %bitcast.174), kind=kLoop, calls=%fused_computation.138 | loop fusion | flops 33554432 | bytes 25264384 | tf_op jit(solution)/shard_map/stack | solution.py:61
  304.1 16.3 %fusion.92 = (bf16[5,8,2,256,1024]{4,3,2,1,0:T(8,128)(2,1)}, bf16[5,8,2,256,1024]{4,3,2,1,0:T(8,128)(2,1)}, bf16[5,8,2,256,1024]{4,3,2,1,0:T(8,128)(2,1)}) fusion(bf16[5,8,2,256,1024]{4,3,2,1,0:T(8,128)(2,1)} %get-tuple-element.23, bf16[8,2,256,1028]{3,2,1,0:T(8,128)(2,1)S(1)} %bitcast.174, bf16[8,2,2,1028]{3,2,1,0:T(2,128)(2,1)S(1)} %collective-permute-done.2, ...), kind=kLoop, calls=%fused_computation.147 | loop fusion | flops 50331648 | bytes 33718784 | tf_op jit(solution)/shard_map/stack | solution.py:61
  343.4 19.8 %fusion.75 = (bf16[5,8,2,256,1024]{4,3,2,1,0:T(8,128)(2,1)}, bf16[5,8,2,256,1024]{4,3,2,1,0:T(8,128)(2,1)}) fusion(bf16[5,8,2,256,1024]{4,3,2,1,0:T(8,128)(2,1)} %fusion.72, bf16[8,2,2,1028]{3,2,1,0:T(2,128)(2,1)S(1)} %collective-permute-done.2, bf16[8,2,256,1028]{3,2,1,0:T(8,128)(2,1)S(1)} %bitcast.174, ...), kind=kLoop, calls=%fused_computation.126 | loop fusion | flops 33554432 | bytes 25330176 | tf_op jit(solution)/shard_map/stack | solution.py:61
  381.3 62.5 %multiply_reduce_fusion.2 = (f32[8,2,256,1024]{3,2,1,0:T(8,128)}, f32[8,2,256,1024]{3,2,1,0:T(8,128)}) fusion(bf16[5,8,2,256,1024]{4,3,2,1,0:T(8,128)(2,1)} %fusion.48, f32[5,8,256,1024]{3,2,1,0:T(8,128)} %get-tuple-element.11, bf16[5,8,2,256,1024]{4,3,2,1,0:T(8,128)(2,1)} %get-tuple-element.25), kind=kLoop, calls=%fused_computation.2 | loop fusion | flops 117440512 | bytes 159383552 | tf_op jit(solution)/shard_map/reduce_sum | solution.py:67
  443.8 11.8 %bitcast_dynamic-update-slice_fusion.4 = f32[5,8,2,256,1024]{4,3,2,1,0:T(8,128)} fusion(f32[8,2,256,1024]{3,2,1,0:T(8,128)} %get-tuple-element.9), kind=kLoop, calls=%fused_computation.42 | loop fusion | bytes 33554432
  455.7 90.3 %multiply_reduce_fusion.1 = (f32[8,2,256,1024]{3,2,1,0:T(8,128)}, f32[8,2,256,1024]{3,2,1,0:T(8,128)}, f32[8,2,256,1024]{3,2,1,0:T(8,128)}) fusion(bf16[5,8,2,256,1024]{4,3,2,1,0:T(8,128)(2,1)} %get-tuple-element.20, f32[5,8,256,1024]{3,2,1,0:T(8,128)} %get-tuple-element.11, bf16[5,8,2,256,1024]{4,3,2,1,0:T(8,128)(2,1)} %get-tuple-element.18, ...), kind=kLoop, calls=%fused_computation.1 | loop fusion | flops 176160768 | bytes 218103808 | tf_op jit(solution)/shard_map/reduce_sum | solution.py:67
  546.0 13.0 %bitcast_dynamic-update-slice_fusion.3 = f32[5,8,2,256,1024]{4,3,2,1,0:T(8,128)} fusion(f32[5,8,2,256,1024]{4,3,2,1,0:T(8,128)} %bitcast_dynamic-update-slice_fusion.4, f32[8,2,256,1024]{3,2,1,0:T(8,128)} %get-tuple-element.6), kind=kLoop, calls=%fused_computation.41 | loop fusion | bytes 33554432
  559.0 13.7 %bitcast_dynamic-update-slice_fusion.2 = f32[5,8,2,256,1024]{4,3,2,1,0:T(8,128)} fusion(f32[5,8,2,256,1024]{4,3,2,1,0:T(8,128)} %bitcast_dynamic-update-slice_fusion.3, f32[8,2,256,1024]{3,2,1,0:T(8,128)} %get-tuple-element.7), kind=kLoop, calls=%fused_computation.40 | loop fusion | bytes 33554432
  589.8 48.2 %multiply_reduce_fusion = f32[8,2,256,1024]{3,2,1,0:T(8,128)} fusion(f32[5,8,2,256,1024]{4,3,2,1,0:T(8,128)} %bitcast_dynamic-update-slice_fusion, f32[5,8,256,1024]{3,2,1,0:T(8,128)} %get-tuple-element.10), kind=kLoop, calls=%fused_computation | loop fusion | flops 37748736 | bytes 142606336 | tf_op jit(solution)/shard_map/reduce_sum | solution.py:68
  638.0 42.0 %fusion.1 = f32[2,256,1024,8]{2,3,1,0:T(8,128)} fusion(f32[8,2,256,1024]{3,2,1,0:T(8,128)} %multiply_reduce_fusion, f32[2,8,8]{2,1,0:T(8,128)S(1)} %copy-done.5), kind=kOutput, calls=%fused_computation.43 | convolution fusion | flops 402653184 | bytes 33554944 | tf_op jit(solution)/shard_map/vlk,kvij->lvij/dot_general | solution.py:69
  680.0 20.8 %fusion.93 = f32[8,2,256,16]{3,0,2,1:T(8,128)} fusion(f32[2,256,1024,8]{2,3,1,0:T(8,128)} %fusion.1, f32[8,2,256,1024]{3,2,1,0:T(8,128)} %multiply_reduce_fusion, f32[2,256,1024]{2,1,0:T(8,128)} %convert_element_type.50, bf16[1024,8]{0,1:T(8,128)(2,1)S(1)} %copy-done.4, bf16[1024,8]{0,1:T(8,128)(2,1)S(1)} %copy-done.3), kind=kOutput, calls=%fused_computation.160 | convolution fusion | flops 146866176 | bytes 35946496 | tf_op jit(solution)/shard_map/dot_general | solution.py:75
  703.7 14.1 %reduce-scatter.2.cloned.1.call-done = f32[4,2,256,16]{2,3,1,0:T(8,128)} async-done(((f32[8,2,256,16]{2,3,1,0:T(8,128)}), f32[4,2,256,16]{2,3,1,0:T(8,128)}) %reduce-scatter.2.cloned.1.call-update) | async-done | bytes 131088 | tf_op jit(solution)/shard_map/reduce_scatter | solution.py:74
  718.8 10.1 %all_to_all.18 = bf16[4,2,256,2,8]{2,3,1,0,4:T(2,128)(2,1)S(1)} all-to-all(bf16[4,2,256,2,8]{2,3,1,0,4:T(2,128)(2,1)S(1)} %copy.29), channel_id=1, replica_groups=mesh['grp'=2,'lat'=4,'lev'=2,'fld'=2] {'lat'}, dimensions={4} | all-to-all | bytes 131072 | tf_op jit(solution)/shard_map/all_to_all | solution.py:89
  (92 shorter events, 157.1 us)
Async XLA Ops:
  6.5 727.5 %copy-start = (bf16[2,1024,512]{2,1,0:T(8,128)(2,1)S(1)}, bf16[2,1024,512]{2,1,0:T(8,128)(2,1)}, u32[]{:S(2)}) copy-start(bf16[2,1024,512]{2,1,0:T(8,128)(2,1)} %param.13) | copy-start | bytes 6291460
  6.5 711.3 %reduce-scatter.2.cloned.1.call-start = ((), (), s32[]{:S(2)}) async-start(), calls=%async_computation.2 | async-start | bytes 393216 | tf_op jit(solution)/shard_map/reduce_scatter | solution.py:74
  11.3 143.0 %collective-permute-start = (bf16[8,2,256,2]{2,0,3,1:T(8,128)(2,1)S(1)}, bf16[8,2,256,2]{2,0,3,1:T(8,128)(2,1)S(1)}, u32[]{:S(2)}, u32[]{:S(2)}) collective-permute-start(bf16[8,2,256,2]{2,0,3,1:T(8,128)(2,1)S(1)} %copy.38), channel_id=1, source_target_pairs={{0,2},{2,0},{1,3},{3,1},{4,6},{6,4},{5,7},{7,5},{8,10},{10,8},{9,1... | collective-permute-start | bytes 49160 | tf_op jit(solution)/shard_map/ppermute | solution.py:19
  14.6 148.6 %collective-permute-start.1 = (bf16[8,2,256,2]{2,0,3,1:T(8,128)(2,1)S(1)}, bf16[8,2,256,2]{2,0,3,1:T(8,128)(2,1)S(1)}, u32[]{:S(2)}, u32[]{:S(2)}) collective-permute-start(bf16[8,2,256,2]{2,0,3,1:T(8,128)(2,1)S(1)} %copy.39), channel_id=1, source_target_pairs={{2,0},{0,2},{3,1},{1,3},{6,4},{4,6},{7,5},{5,7},{10,8},{8,10},{11,... | collective-permute-start | bytes 49160 | tf_op jit(solution)/shard_map/ppermute | solution.py:20
  14.7 44.3 %slice-start.3 = ((s8[8388608]{0:T(1024)(128)(4,1)}), s8[4194304]{0:T(1024)(128)(4,1)S(1)}, s32[]{:S(2)}) async-start(s8[8388608]{0:T(1024)(128)(4,1)} %bitcast.175), calls=%async_computation.6 | async-start | bytes 8388608
  14.7 44.3 %slice-start.5 = ((s8[8388608]{0:T(1024)(128)(4,1)}), s8[4194304]{0:T(1024)(128)(4,1)S(1)}, s32[]{:S(2)}) async-start(s8[8388608]{0:T(1024)(128)(4,1)} %bitcast.177), calls=%async_computation.8 | async-start | bytes 8388608
  31.4 27.7 %slice-start.4 = ((s8[8388608]{0:T(1024)(128)(4,1)}), s8[4194304]{0:T(1024)(128)(4,1)S(1)}, s32[]{:S(2)}) async-start(s8[8388608]{0:T(1024)(128)(4,1)} %bitcast.175), calls=%async_computation.7 | async-start | bytes 8388608
  31.4 27.7 %slice-start.6 = ((s8[8388608]{0:T(1024)(128)(4,1)}), s8[4194304]{0:T(1024)(128)(4,1)S(1)}, s32[]{:S(2)}) async-start(s8[8388608]{0:T(1024)(128)(4,1)} %bitcast.177), calls=%async_computation.9 | async-start | bytes 8388608
  111.4 13.0 %copy-start.6 = (s32[8]{0:T(128)S(1)}, s32[8]{0:T(128)}, u32[]{:S(2)}) copy-start(s32[8]{0:T(128)} %param.12) | copy-start | bytes 100
  124.4 28.3 %copy-start.2 = (bf16[2,256,1024]{2,1,0:T(8,128)(2,1)S(1)}, bf16[2,256,1024]{2,1,0:T(8,128)(2,1)}, u32[]{:S(2)}) copy-start(bf16[2,256,1024]{2,1,0:T(8,128)(2,1)} %param.10) | copy-start | bytes 3145732
  183.2 47.1 %collective-permute-start.2 = (bf16[8,2,2,1028]{3,2,1,0:T(2,128)(2,1)S(1)}, bf16[8,2,2,1028]{3,2,1,0:T(2,128)(2,1)S(1)}, u32[]{:S(2)}, u32[]{:S(2)}) collective-permute-start(bf16[8,2,2,1028]{3,2,1,0:T(2,128)(2,1)S(1)} %get-tuple-element.27), channel_id=1, source_target_pairs={{0,4},{4,8},{8,12},{1,5},{5,9},{9,13},{2,6},{6,10},{10,14},{3,7},{... | collective-permute-start | bytes 197384 | tf_op jit(solution)/shard_map/ppermute | solution.py:19
  187.2 71.2 %collective-permute-start.3 = (bf16[8,2,2,1028]{3,2,1,0:T(2,128)(2,1)S(1)}, bf16[8,2,2,1028]{3,2,1,0:T(2,128)(2,1)S(1)}, u32[]{:S(2)}, u32[]{:S(2)}) collective-permute-start(bf16[8,2,2,1028]{3,2,1,0:T(2,128)(2,1)S(1)} %get-tuple-element.28), channel_id=1, source_target_pairs={{4,0},{8,4},{12,8},{5,1},{9,5},{13,9},{6,2},{10,6},{14,10},{7,3},{... | collective-permute-start | bytes 197384 | tf_op jit(solution)/shard_map/ppermute | solution.py:20
  230.4 20.0 %slice-start = ((s8[9437184]{0:T(1024)(128)(4,1)}), s8[4194304]{0:T(1024)(128)(4,1)S(1)}, s32[]{:S(2)}) async-start(s8[9437184]{0:T(1024)(128)(4,1)} %bitcast.173), calls=%async_computation.3 | async-start | bytes 8388608
  230.4 20.0 %slice-start.1 = ((s8[9437184]{0:T(1024)(128)(4,1)}), s8[4194304]{0:T(1024)(128)(4,1)S(1)}, s32[]{:S(2)}) async-start(s8[9437184]{0:T(1024)(128)(4,1)} %bitcast.173), calls=%async_computation.4 | async-start | bytes 8388608
  546.0 26.7 %slice-start.7 = ((s8[16777216]{0:T(1024)(128)(4,1)}), s8[4194304]{0:T(1024)(128)(4,1)S(1)}, s32[]{:S(2)}) async-start(s8[16777216]{0:T(1024)(128)(4,1)} %bitcast.179), calls=%async_computation.10 | async-start | bytes 8388608
  546.0 26.7 %slice-start.8 = ((s8[16777216]{0:T(1024)(128)(4,1)}), s8[4194304]{0:T(1024)(128)(4,1)S(1)}, s32[]{:S(2)}) async-start(s8[16777216]{0:T(1024)(128)(4,1)} %bitcast.179), calls=%async_computation.11 | async-start | bytes 8388608
  559.0 13.7 %slice-start.9 = ((s8[16777216]{0:T(1024)(128)(4,1)}), s8[4194304]{0:T(1024)(128)(4,1)S(1)}, s32[]{:S(2)}) async-start(s8[16777216]{0:T(1024)(128)(4,1)} %bitcast.179), calls=%async_computation.12 | async-start | bytes 8388608
  559.0 13.8 %slice-start.10 = ((s8[16777216]{0:T(1024)(128)(4,1)}), s8[4194304]{0:T(1024)(128)(4,1)S(1)}, s32[]{:S(2)}) async-start(s8[16777216]{0:T(1024)(128)(4,1)} %bitcast.179), calls=%async_computation.13 | async-start | bytes 8388608
  559.0 22.2 %slice-start.11 = ((s8[16777216]{0:T(1024)(128)(4,1)}), s8[4194304]{0:T(1024)(128)(4,1)S(1)}, s32[]{:S(2)}) async-start(s8[16777216]{0:T(1024)(128)(4,1)} %bitcast.181), calls=%async_computation.14 | async-start | bytes 8388608
  559.0 22.2 %slice-start.12 = ((s8[16777216]{0:T(1024)(128)(4,1)}), s8[4194304]{0:T(1024)(128)(4,1)S(1)}, s32[]{:S(2)}) async-start(s8[16777216]{0:T(1024)(128)(4,1)} %bitcast.181), calls=%async_computation.15 | async-start | bytes 8388608
  572.8 11.0 %slice-start.14 = ((s8[16777216]{0:T(1024)(128)(4,1)}), s8[4194304]{0:T(1024)(128)(4,1)S(1)}, s32[]{:S(2)}) async-start(s8[16777216]{0:T(1024)(128)(4,1)} %bitcast.181), calls=%async_computation.17 | async-start | bytes 8388608
  589.8 48.2 %copy-start.5 = (f32[2,8,8]{2,1,0:T(8,128)S(1)}, f32[2,8,8]{2,1,0:T(8,128)}, u32[]{:S(2)}) copy-start(f32[2,8,8]{2,1,0:T(8,128)} %param.11) | copy-start | bytes 1540
  638.0 42.0 %copy-start.3 = (bf16[1024,8]{0,1:T(8,128)(2,1)S(1)}, bf16[1024,8]{0,1:T(8,128)(2,1)}, u32[]{:S(2)}) copy-start(bf16[1024,8]{0,1:T(8,128)(2,1)} %get-tuple-element.31) | copy-start | bytes 49156
  638.0 42.0 %copy-start.4 = (bf16[1024,8]{0,1:T(8,128)(2,1)S(1)}, bf16[1024,8]{0,1:T(8,128)(2,1)}, u32[]{:S(2)}) copy-start(bf16[1024,8]{0,1:T(8,128)(2,1)} %get-tuple-element.32) | copy-start | bytes 49156
  (3 other events, 28.5 us)
Sparse Core Ops, SparseCore 0:
  703.8 13.9 reduce-scatter.1
where the time goes:
time: 751 us; the launch traced here: 742 us
  other arithmetic  534 us (71%)
  local copies, waits for them, and re-layouts  93 us (12%)
  matrix products  63.2 us (8%)
  blocking collectives  15.1 us (2%)
  waiting for transfers between devices  14.2 us (2%)
  between operations  13.8 us (2%)
  starting transfers between devices  8.47 us (1%)
    unnamed x24, other arithmetic  235 us
    reduce_sum x2, other arithmetic, shards(): jnp.sum(windows.astype(jnp.float32) * col_weights[:, :, None], axis=0)  153 us
    another operation x5, other arithmetic, shards(): jnp.stack([padded[:, :, row_off:row_off + lat_dev, col_off:col_off + lon_...  67.2 us
    unnamed x51, local copies, waits for them, and re-layouts  59.6 us
    reduce_sum x1, other arithmetic, shards(): interp = jnp.sum(jnp.stack(row_sums) * row_weights[:, :, None], axis=0)  48.2 us
    dot_general x1, matrix products, shards(): jnp.einsum('vlk,kvij->lvij', mixing, interp, precision=lax.Precision.HIGH...  42 us
    another operation x1, other arithmetic, offset_weights(): return jnp.stack(result)  27.5 us
    dot_general x1, matrix products, shards(): jnp.dot(state.reshape(-1, lon_dev), local_basis, preferred_element_type=j...  20.8 us
  transfers between devices with their start and end apart: 5, of which 1 were waited for; matrix products, arithmetic and copies ran while one was open for 29% of the time, Pallas kernels for 0%

commit v1 on v0

--- a/solution.py
+++ b/solution.py
@@ -3,10 +3,15 @@
 import jax
 import jax.numpy as jnp
 from jax import lax
+from jax.experimental import pallas as pl
+from jax.experimental.pallas import tpu as pltpu
 from jax.sharding import PartitionSpec as P
 
 NLON = 2048
 NTRUNC = 1024
+ROWS = 32
+BLOCKS = 8
+LANES = 128
 
 
 def with_halo(shard, sides, width, wrap):
@@ -48,7 +53,7 @@
     return jnp.concatenate([jnp.cos(angle), -jnp.sin(angle)], axis=1).astype(jnp.bfloat16)
 
 
-def shards(upstream, departure, fractions, heating, mixing, slot_wavenumber, legendre):
+def shards_plain(upstream, departure, fractions, heating, mixing, slot_wavenumber, legendre):
     levels, var_dev, lat_dev, lon_dev = upstream.shape
     widened = with_halo(upstream, (("lev", 3),), 2, True)
     padded = with_halo(widened, (("lat", 2),), 2, False)
@@ -95,6 +100,243 @@
     )
 
 
+def axis_weights(x):
+    square = x * x
+    cubic = x * (square - 1.0) * (1.0 / 6.0)
+    right = jnp.where(x > 0.0, cubic, 0.0)
+    half = 0.5 * square
+    half_x = 0.5 * x
+    inner = half - 4.0 * right
+    triple = 3.0 * cubic
+    return [
+        right - cubic,
+        inner + (triple - half_x),
+        (1.0 - square) + (6.0 * right - triple),
+        inner + (half_x + cubic),
+        right,
+    ]
+
+
+def column_kernel(
+    main, prev, following, e_main, e_prev, e_following, top, bottom, departure, fractions,
+    heating, coupling, basis, out, turned, edges, images, nearest, position, interp, state,
+):
+    levels, variables = main.shape[0], main.shape[1]
+    rows = main.shape[2]
+    pack = variables * BLOCKS
+    block = pl.program_id(0)
+    first = block == 0
+    last = block == pl.num_programs(0) - 1
+    lane = lax.broadcasted_iota(jnp.int32, (variables, BLOCKS, LANES), 2)
+    sub = lax.broadcasted_iota(jnp.int32, (variables, BLOCKS, LANES), 1)
+
+    def turn(values, start, v):
+        count = values.shape[0]
+        for jb in range(BLOCKS):
+            turned[pl.ds(start * pack + v * BLOCKS + jb, count, stride=pack), :] = values[
+                :, jb * LANES : (jb + 1) * LANES
+            ]
+
+    def one_level(l, carry):
+        for v in range(variables):
+            width = BLOCKS * LANES
+            turn(main[l, v].astype(jnp.float32), 8, v)
+            before = prev[l, v].astype(jnp.float32)[8:16]
+            turn(jnp.where(first, top[l, v, :, :width], before), 0, v)
+            after = following[l, v].astype(jnp.float32)[0:8]
+            turn(jnp.where(last, bottom[l, v, :, :width], after), 8 + rows, v)
+            edges[v, 8 : 8 + rows] = e_main[l, v].astype(jnp.float32)
+            before = e_prev[l, v].astype(jnp.float32)[8:16]
+            edges[v, 0:8] = jnp.where(first, top[l, v, :, width:], before)
+            after = e_following[l, v].astype(jnp.float32)[0:8]
+            edges[v, 8 + rows : 16 + rows] = jnp.where(last, bottom[l, v, :, width:], after)
+        code = departure[l]
+        t_lat = fractions[0, l].astype(jnp.float32)
+        t_lon = fractions[1, l].astype(jnp.float32)
+        y = jnp.where(code >= 2, t_lat, t_lat - 1.0)
+        x = jnp.where((code & 1) == 1, t_lon, t_lon - 1.0)
+        for jb in range(BLOCKS):
+            lanes = slice(jb * LANES, (jb + 1) * LANES)
+            position[0, pl.ds(jb, rows, stride=BLOCKS), :] = y[:, lanes]
+            position[1, pl.ds(jb, rows, stride=BLOCKS), :] = x[:, lanes]
+
+        def make_images(w, carry):
+            at = pl.multiple_of((w + 6) * pack, pack)
+            values = turned[pl.ds(at, pack), :].reshape(variables, BLOCKS, LANES)
+            edge = jnp.stack(
+                [
+                    jnp.broadcast_to(edges[v, pl.ds(w + 6, 1), :], (BLOCKS, LANES))
+                    for v in range(variables)
+                ]
+            )
+            ahead = jnp.where(sub == BLOCKS - 1, edge, pltpu.roll(values, BLOCKS - 1, 1))
+            behind = jnp.where(sub == 0, edge, pltpu.roll(values, 1, 1))
+            shifted = [
+                pltpu.roll(jnp.where(lane >= LANES - 2, behind, values), 2, 2),
+                pltpu.roll(jnp.where(lane >= LANES - 1, behind, values), 1, 2),
+                values,
+                pltpu.roll(jnp.where(lane < 1, ahead, values), LANES - 1, 2),
+                pltpu.roll(jnp.where(lane < 2, ahead, values), LANES - 2, 2),
+            ]
+            for q in range(5):
+                image = shifted[q].reshape(pack, LANES)
+                images[q, w] = image.astype(jnp.bfloat16)
+                if q in (1, 2, 3):
+                    nearest[q - 1, w] = image
+            return carry
+
+        lax.fori_loop(0, rows + 4, make_images, 0, unroll=4)
+
+        def interpolate(i, carry):
+            at = pl.multiple_of(i * BLOCKS, BLOCKS)
+            row_w = axis_weights(position[0, pl.ds(at, BLOCKS), :])
+            col_w = axis_weights(position[1, pl.ds(at, BLOCKS), :])
+            row_w = [jnp.concatenate([w] * variables, axis=0) for w in row_w]
+            col_w = [jnp.concatenate([w] * variables, axis=0) for w in col_w]
+            row_n = [w.astype(jnp.bfloat16) for w in row_w]
+            col_n = [w.astype(jnp.bfloat16) for w in col_w]
+            outer = inner = None
+            for r in range(5):
+                line = col_n[0] * images[0, i + r] + col_n[4] * images[4, i + r]
+                if r in (0, 4):
+                    middle = [col_n[q] * images[q, i + r] for q in (1, 2, 3)]
+                    line = (middle[0] + middle[1]) + (middle[2] + line)
+                else:
+                    near = [col_w[q] * nearest[q - 1, i + r] for q in (1, 2, 3)]
+                    near = row_w[r] * (near[0] + near[1] + near[2])
+                    inner = near if inner is None else inner + near
+                line = row_n[r] * line
+                outer = line if outer is None else outer + line
+            total = inner + outer.astype(jnp.float32)
+            interp[l, pl.ds(pl.multiple_of(i * pack, pack), pack), :] = total
+            return carry
+
+        lax.fori_loop(0, rows, interpolate, 0, unroll=4)
+        return carry
+
+    lax.fori_loop(0, levels, one_level, 0)
+
+    for v in range(variables):
+        for jb in range(BLOCKS):
+            lanes = slice(jb * LANES, (jb + 1) * LANES)
+            field = jnp.concatenate(
+                [interp[l, pl.ds(v * BLOCKS + jb, rows, stride=pack), :] for l in range(levels)],
+                axis=0,
+            )
+            column = jnp.dot(
+                coupling[v], field.astype(jnp.bfloat16), preferred_element_type=jnp.float32
+            )
+            heat = jnp.concatenate([heating[v, :, lanes].astype(jnp.float32)] * levels, axis=0)
+            state[:, lanes] = (field + heat * jnp.tanh(column)).astype(jnp.bfloat16)
+        out[v, 0] = lax.dot_general(
+            basis[...], state[...], (((1,), (1,)), ((), ())), preferred_element_type=jnp.float32
+        )
+
+
+def step_sums(upstream, departure, fractions, heating, mixing, basis):
+    levels, variables, lat_dev, lon_dev = upstream.shape
+    rows, near = ROWS, 16
+    steps = lat_dev // rows
+    peers = lax.axis_size("lev")
+    up = [(i, (i + 1) % peers) for i in range(peers)]
+    down = [(j, i) for i, j in up]
+    left = lax.ppermute(upstream[..., lon_dev - 2 :], "lev", up)
+    right = lax.ppermute(upstream[..., :2], "lev", down)
+    gap = jnp.zeros((levels, variables, lat_dev, LANES - 4), upstream.dtype)
+    edge = jnp.concatenate([right, gap, left], axis=3)
+    bands = lax.axis_size("lat")
+    north = [(i, i + 1) for i in range(bands - 1)]
+    south = [(j, i) for i, j in north]
+    lower = jnp.concatenate([upstream[:, :, lat_dev - 2 :], edge[:, :, lat_dev - 2 :]], axis=3)
+    upper = jnp.concatenate([upstream[:, :, :2], edge[:, :, :2]], axis=3)
+    top = lax.ppermute(lower, "lat", north).astype(jnp.float32)
+    bottom = lax.ppermute(upper, "lat", south).astype(jnp.float32)
+    top = jnp.pad(top, ((0, 0), (0, 0), (6, 0), (0, 0)))
+    bottom = jnp.pad(bottom, ((0, 0), (0, 0), (0, 6), (0, 0)))
+    unit = jnp.eye(rows, dtype=jnp.float32)
+    coupling = (mixing[:, :, None, :, None] * unit[None, None, :, None, :]).reshape(
+        variables, levels * rows, levels * rows
+    )
+    ratio = rows // near
+    ends = lat_dev // near - 1
+
+    def around(width):
+        return [
+            pl.BlockSpec((levels, variables, rows, width), lambda b: (0, 0, b, 0)),
+            pl.BlockSpec(
+                (levels, variables, near, width),
+                lambda b: (0, 0, jnp.maximum(b * ratio - 1, 0), 0),
+            ),
+            pl.BlockSpec(
+                (levels, variables, near, width),
+                lambda b: (0, 0, jnp.minimum((b + 1) * ratio, ends), 0),
+            ),
+        ]
+
+    def whole(shape):
+        return pl.BlockSpec(shape, lambda b: (0,) * len(shape))
+
+    pack = variables * BLOCKS
+    slots = basis.shape[0]
+    return pl.pallas_call(
+        column_kernel,
+        grid=(steps,),
+        out_shape=jax.ShapeDtypeStruct((variables, steps, slots, levels * rows), jnp.float32),
+        in_specs=around(lon_dev)
+        + around(LANES)
+        + [
+            whole(top.shape),
+            whole(bottom.shape),
+            pl.BlockSpec((levels, rows, lon_dev), lambda b: (0, b, 0)),
+            pl.BlockSpec((2, levels, rows, lon_dev), lambda b: (0, 0, b, 0)),
+            pl.BlockSpec((variables, rows, lon_dev), lambda b: (0, b, 0)),
+            whole(coupling.shape),
+            whole(basis.shape),
+        ],
+        out_specs=pl.BlockSpec((variables, 1, slots, levels * rows), lambda b: (0, b, 0, 0)),
+        scratch_shapes=[
+            pltpu.VMEM(((rows + 16) * pack, LANES), jnp.float32),
+            pltpu.VMEM((variables, rows + 16, LANES), jnp.float32),
+            pltpu.VMEM((5, rows + 4, pack, LANES), jnp.bfloat16),
+            pltpu.VMEM((3, rows + 4, pack, LANES), jnp.float32),
+            pltpu.VMEM((2, rows * BLOCKS, LANES), jnp.float32),
+            pltpu.VMEM((levels, rows * pack, LANES), jnp.float32),
+            pltpu.VMEM((levels * rows, lon_dev), jnp.bfloat16),
+        ],
+        compiler_params=pltpu.CompilerParams(vmem_limit_bytes=48 * 1024 * 1024),
+    )(
+        upstream, upstream, upstream, edge, edge, edge, top, bottom, departure, fractions,
+        heating, coupling.astype(jnp.bfloat16), basis,
+    )
+
+
+def shards(upstream, departure, fractions, heating, mixing, slot_wavenumber, legendre):
+    levels, var_dev, lat_dev, lon_dev = upstream.shape
+    if lon_dev != BLOCKS * LANES or lat_dev % ROWS or var_dev * BLOCKS != 16:
+        return shards_plain(
+            upstream, departure, fractions, heating, mixing, slot_wavenumber, legendre
+        )
+    m_window = slot_wavenumber.shape[0]
+    waves = slot_wavenumber * (NTRUNC // m_window)
+    basis = fourier_basis(lax.axis_index("lev") * lon_dev, lon_dev, waves).T
+    partial = step_sums(upstream, departure, fractions, heating, mixing, basis)
+    partial = partial.reshape(var_dev, lat_dev // ROWS, 2 * m_window, levels, ROWS)
+    partial = partial.transpose(3, 0, 1, 4, 2).reshape(levels, var_dev, lat_dev, 2 * m_window)
+    sums = lax.psum_scatter(partial, "lev", scatter_dimension=0, tiled=True)
+    coefficients = (
+        (sums * (1.0 / math.sqrt(NLON)))
+        .astype(jnp.bfloat16)
+        .reshape(-1, var_dev, lat_dev, 2, m_window)
+    )
+    owned = lax.all_to_all(coefficients, "lat", split_axis=4, concat_axis=2, tiled=True)
+    return jnp.einsum(
+        "sin,lvirs->snrvl",
+        legendre,
+        lax.all_gather(owned, "lev", axis=0, tiled=True),
+        preferred_element_type=jnp.float32,
+    )
+
+
 def solution(mesh):
     in_specs = (
         P("grp", "fld", "lat", "lev"),

time: 751 us -> 204 us (0.27); the launches traced: 742 us -> 204 us
  other arithmetic: 534 us -> 4.54 us
  Pallas kernels: 0 us -> 126 us
  local copies, waits for them, and re-layouts: 93 us -> 19.1 us
  matrix products: 63.2 us -> 0.41 us
    unnamed x24 -> x0, other arithmetic: 235 us -> none
    reduce_sum x3 -> x0, other arithmetic: 201 us -> none  [the longest x2 153 us: shards(): jnp.sum(windows.astype(jnp.float32) * col_weights[:, :, None], axis=0)]
    pallas_call x0 -> x1, Pallas kernels: none -> 126 us  [step_sums(): pl.pallas_call(column_kernel, grid=(steps,), out_shape=jax.ShapeDtypeStru...]
    another operation x7 -> x1, other arithmetic: 95.4 us -> 0.22 us  [the longest x5 67.2 us: shards(): jnp.stack([padded[:, :, row_off:row_off + lat_dev, col_off:col_off + lon_...]
    dot_general x2 -> x0, matrix products: 62.8 us -> none  [the longest x1 42 us: shards(): jnp.einsum('vlk,kvij->lvij', mixing, interp, precision=lax.Precision.HIGH...]
    unnamed x51 -> x18, local copies, waits for them, and re-layouts: 59.6 us -> 2.01 us
    concatenate x1, local copies, waits for them, and re-layouts: 17.4 us -> 0.6 us  [step_sums(): edge = jnp.concatenate([right, gap, left], axis=3)]
  transfers between devices with their start and end apart: 5 -> 5, of which waited for: 1 -> 3; matrix products, arithmetic and copies ran while one was open for 29% -> 5% of each run, Pallas kernels for 0% -> 0%
where the time goes in v1:
time: 204 us
  Pallas kernels  126 us (62%)
  local copies, waits for them, and re-layouts  19.1 us (9%)
  waiting for transfers between devices  16.2 us (8%)
  blocking collectives  15.1 us (7%)
  between operations  13.6 us (7%)
  starting transfers between devices  8.97 us (4%)
  other arithmetic  4.54 us (2%)
    pallas_call x1, Pallas kernels, step_sums(): pl.pallas_call(column_kernel, grid=(steps,), out_shape=jax.ShapeDtypeStru...  126 us
    reduce_scatter x1, waiting for transfers between devices, shards(): sums = lax.psum_scatter(partial, 'lev', scatter_dimension=0, tiled=True)  14.3 us
    all_to_all x1, blocking collectives, shards(): lax.all_to_all(coefficients, 'lat', split_axis=4, concat_axis=2, tiled=True)  10.1 us
    all_gather x1, blocking collectives, shards(): lax.all_gather(owned, 'lev', axis=0, tiled=True)  4.94 us
    ppermute x1, starting transfers between devices, step_sums(): top = lax.ppermute(lower, 'lat', north).astype(jnp.float32)  4.62 us
  transfers between devices with their start and end apart: 5, of which 3 were waited for; matrix products, arithmetic and copies ran while one was open for 5% of the time, Pallas kernels for 0%

profile of v1, /device:TPU:0, one launch (start us, length us, event | category | flops | bytes accessed | tf_op | source)
XLA Modules:
  0.0 203.8 jit_solution(16042194812306669612)
XLA Ops:
  6.5 3.1 %fusion.12 = (bf16[8,2,256,2]{3,2,1,0:T(8,128)(2,1)S(1)}, bf16[8,2,256,2]{3,2,1,0:T(8,128)(2,1)}) fusion(bf16[8,2,256,1024]{3,2,1,0:T(8,128)(2,1)} %following.1), kind=kLoop, calls=%fused_computation.29 | loop fusion | bytes 65536 | tf_op jit(solution)/shard_map/slice | solution.py:244
  9.7 1.6 copy.35
  11.3 3.0 %collective-permute-start.1 = (bf16[8,2,256,2]{2,0,3,1:T(8,128)(2,1)S(1)}, bf16[8,2,256,2]{2,0,3,1:T(8,128)(2,1)S(1)}, u32[]{:S(2)}, u32[]{:S(2)}) collective-permute-start(bf16[8,2,256,2]{2,0,3,1:T(8,128)(2,1)S(1)} %copy.35), channel_id=1, source_target_pairs={{0,2},{2,0},{1,3},{3,1},{4,6},{6,4},{5,7},{7,5},{8,10},{10,8},{9,1... | collective-permute-start | bytes 49160 | tf_op jit(solution)/shard_map/ppermute | solution.py:243
  14.7 1.8 fusion.11
  16.5 0.5 broadcast_multiply_fusion
  17.0 0.6 iota_add_fusion
  18.0 1.5 mul.51
  19.5 2.1 %mul.52 = f32[2,256,256]{2,1,0:T(8,128)S(1)} reshape(f32[2,8,32,8,32]{4,3,2,1,0:T(8,128)} %mul.51) | data formatting | bytes 1048576 | tf_op jit(solution)/shard_map/mul | solution.py:257
  22.0 0.6 pad.23.clone
  22.6 1.2 copy.24
  23.8 1.4 copy.25
  25.2 2.0 pad_maximum_fusion.e_main.e_prev.e_following
  27.3 1.3 collective-permute-start.3
  28.7 4.6 %collective-permute-start.2 = (bf16[8,2,2,1152]{3,2,1,0:T(2,128)(2,1)S(1)}, bf16[8,2,2,1152]{3,2,1,0:T(2,128)(2,1)S(1)}, u32[]{:S(2)}, u32[]{:S(2)}) collective-permute-start(bf16[8,2,2,1152]{3,2,1,0:T(2,128)(2,1)S(1)} %pad_maximum_fusion.1), channel_id=1, source_target_pairs={{0,4},{4,8},{8,12},{1,5},{5,9},{9,13},{2,6},{6,10},{10,14},{3,7},{... | collective-permute-start | bytes 221192 | tf_op jit(solution)/shard_map/ppermute | solution.py:252
  33.7 1.6 collective-permute-done.2
  35.4 125.9 %shard_map.73 = f32[2,8,16,256]{3,2,1,0:T(8,128)S(1)} custom-call(bf16[8,2,256,1024]{3,2,1,0:T(8,128)(2,1)} %following.1, bf16[8,2,256,1024]{3,2,1,0:T(8,128)(2,1)} %following.1, bf16[8,2,256,1024]{3,2,1,0:T(8,128)(2,1)} %following.1, bf16[8,2,256,128]{3,2,1,0:T(8,128)(2,1)S(1)} %pad_maximum_fusion.e_main.e_prev.e_following, ...), custom_call_target="tpu_custom_call" | custom-call | tf_op jit(solution)/shard_map/pallas_call | solution.py:281
  161.3 1.3 reshape.26
  162.5 1.8 copy.39
  164.4 1.0 reshape.27
  165.4 14.3 %reduce-scatter.2.cloned.1.call-done = f32[4,2,256,16]{2,3,1,0:T(8,128)} async-done(((f32[8,2,256,16]{2,3,1,0:T(8,128)}), f32[4,2,256,16]{2,3,1,0:T(8,128)}) %reduce-scatter.2.cloned.1.call-update) | async-done | bytes 131088 | tf_op jit(solution)/shard_map/reduce_scatter | solution.py:325
  179.7 0.9 fusion.6
  180.7 10.1 %all_to_all.18 = bf16[4,2,256,2,8]{2,3,1,0,4:T(2,128)(2,1)S(1)} all-to-all(bf16[4,2,256,2,8]{2,3,1,0,4:T(2,128)(2,1)S(1)} %copy.27), channel_id=1, replica_groups=mesh['grp'=2,'lat'=4,'lev'=2,'fld'=2] {'lat'}, dimensions={4} | all-to-all | bytes 131072 | tf_op jit(solution)/shard_map/all_to_all | solution.py:331
  190.9 4.9 %all_gather.3 = bf16[8,2,1024,2,2]{2,4,3,1,0:T(2,128)(2,1)S(1)} all-gather(bf16[4,2,1024,2,2]{2,4,3,1,0:T(2,128)(2,1)S(1)} %all_to_all.16), channel_id=1, replica_groups=mesh['grp'=2,'lat'=4,'lev'=2,'fld'=2] {'lev'}, dimensions={0}, use_global_device_ids=true | all-gather | bytes 196608 | tf_op jit(solution)/shard_map/all_gather | solution.py:335
  196.3 0.7 copy.31
  (39 shorter events, 2.3 us)
Async XLA Ops:
  6.5 189.3 %copy-start = (bf16[2,1024,512]{2,1,0:T(8,128)(2,1)S(1)}, bf16[2,1024,512]{2,1,0:T(8,128)(2,1)}, u32[]{:S(2)}) copy-start(bf16[2,1024,512]{2,1,0:T(8,128)(2,1)} %param.13) | copy-start | bytes 6291460
  6.5 173.2 %reduce-scatter.2.cloned.1.call-start = ((), (), s32[]{:S(2)}) async-start(), calls=%async_computation.2 | async-start | bytes 393216 | tf_op jit(solution)/shard_map/reduce_scatter | solution.py:325
  9.7 6.8 %copy-start.7 = (s32[8]{0:T(128)S(1)}, s32[8]{0:T(128)}, u32[]{:S(2)}) copy-start(s32[8]{0:T(128)} %param.12) | copy-start | bytes 100
  11.3 6.7 %copy-start.4 = (f32[2,8,8]{2,1,0:T(8,128)S(1)}, f32[2,8,8]{2,1,0:T(8,128)}, u32[]{:S(2)}) copy-start(f32[2,8,8]{2,1,0:T(8,128)} %param.11) | copy-start | bytes 1540
  11.3 12.6 %collective-permute-start.1 = (bf16[8,2,256,2]{2,0,3,1:T(8,128)(2,1)S(1)}, bf16[8,2,256,2]{2,0,3,1:T(8,128)(2,1)S(1)}, u32[]{:S(2)}, u32[]{:S(2)}) collective-permute-start(bf16[8,2,256,2]{2,0,3,1:T(8,128)(2,1)S(1)} %copy.35), channel_id=1, source_target_pairs={{0,2},{2,0},{1,3},{3,1},{4,6},{6,4},{5,7},{7,5},{8,10},{10,8},{9,1... | collective-permute-start | bytes 49160 | tf_op jit(solution)/shard_map/ppermute | solution.py:243
  14.6 8.0 %collective-permute-start = (bf16[8,2,256,2]{2,0,3,1:T(8,128)(2,1)S(1)}, bf16[8,2,256,2]{2,0,3,1:T(8,128)(2,1)}, u32[]{:S(2)}, u32[]{:S(2)}) collective-permute-start(bf16[8,2,256,2]{2,0,3,1:T(8,128)(2,1)S(1)} %copy.34), channel_id=1, source_target_pairs={{2,0},{0,2},{3,1},{1,3},{6,4},{4,6},{7,5},{5,7},{10,8},{8,10},{11,... | collective-permute-start | bytes 49160 | tf_op jit(solution)/shard_map/ppermute | solution.py:244
  18.0 3.7 %copy-start.3 = (s32[1024]{0:T(1024)S(1)}, s32[1024]{0:T(1024)}, u32[]{:S(2)}) copy-start(s32[1024]{0:T(1024)} %iota_add_fusion) | copy-start | bytes 12292
  18.0 3.7 %copy-start.5 = (s32[8]{0:T(128)S(1)}, s32[8]{0:T(128)}, u32[]{:S(2)}) copy-start(s32[8]{0:T(128)} %broadcast_multiply_fusion) | copy-start | bytes 100
  22.6 2.6 %copy-start.6 = (bf16[128]{0:T(256)(128)(2,1)S(1)}, bf16[128]{0:T(256)(128)(2,1)}, u32[]{:S(2)}) copy-start(bf16[128]{0:T(256)(128)(2,1)} %pad.23.clone) | copy-start | bytes 772
  25.2 2.0 copy-start.2
  25.2 10.1 %copy-start.1 = (bf16[2,256,1024]{2,1,0:T(8,128)(2,1)S(1)}, bf16[2,256,1024]{2,1,0:T(8,128)(2,1)}, u32[]{:S(2)}) copy-start(bf16[2,256,1024]{2,1,0:T(8,128)(2,1)} %heating.1) | copy-start | bytes 3145732
  27.3 6.3 %collective-permute-start.3 = (bf16[8,2,2,1152]{3,2,1,0:T(2,128)(2,1)S(1)}, bf16[8,2,2,1152]{3,2,1,0:T(2,128)(2,1)S(1)}, u32[]{:S(2)}, u32[]{:S(2)}) collective-permute-start(bf16[8,2,2,1152]{3,2,1,0:T(2,128)(2,1)S(1)} %pad_maximum_fusion.2), channel_id=1, source_target_pairs={{4,0},{8,4},{12,8},{5,1},{9,5},{13,9},{6,2},{10,6},{14,10},{7,3},{... | collective-permute-start | bytes 221192 | tf_op jit(solution)/shard_map/ppermute | solution.py:253
  28.7 6.6 %collective-permute-start.2 = (bf16[8,2,2,1152]{3,2,1,0:T(2,128)(2,1)S(1)}, bf16[8,2,2,1152]{3,2,1,0:T(2,128)(2,1)S(1)}, u32[]{:S(2)}, u32[]{:S(2)}) collective-permute-start(bf16[8,2,2,1152]{3,2,1,0:T(2,128)(2,1)S(1)} %pad_maximum_fusion.1), channel_id=1, source_target_pairs={{0,4},{4,8},{8,12},{1,5},{5,9},{9,13},{2,6},{6,10},{10,14},{3,7},{... | collective-permute-start | bytes 221192 | tf_op jit(solution)/shard_map/ppermute | solution.py:252
Sparse Core Ops, SparseCore 0:
  165.5 14.1 reduce-scatter.1

commit v2 on v1

--- a/solution.py
+++ b/solution.py
@@ -12,6 +12,7 @@
 ROWS = 32
 BLOCKS = 8
 LANES = 128
+PITCH = 9
 
 
 def with_halo(shard, sides, width, wrap):
@@ -133,7 +134,7 @@
     def turn(values, start, v):
         count = values.shape[0]
         for jb in range(BLOCKS):
-            turned[pl.ds(start * pack + v * BLOCKS + jb, count, stride=pack), :] = values[
+            turned[v, pl.ds(start * PITCH + jb, count, stride=PITCH), :] = values[
                 :, jb * LANES : (jb + 1) * LANES
             ]
 
@@ -157,12 +158,12 @@
         x = jnp.where((code & 1) == 1, t_lon, t_lon - 1.0)
         for jb in range(BLOCKS):
             lanes = slice(jb * LANES, (jb + 1) * LANES)
-            position[0, pl.ds(jb, rows, stride=BLOCKS), :] = y[:, lanes]
-            position[1, pl.ds(jb, rows, stride=BLOCKS), :] = x[:, lanes]
+            position[0, pl.ds(jb, rows, stride=PITCH), :] = y[:, lanes]
+            position[1, pl.ds(jb, rows, stride=PITCH), :] = x[:, lanes]
 
         def make_images(w, carry):
-            at = pl.multiple_of((w + 6) * pack, pack)
-            values = turned[pl.ds(at, pack), :].reshape(variables, BLOCKS, LANES)
+            at = (w + 6) * PITCH
+            values = jnp.stack([turned[v, pl.ds(at, BLOCKS), :] for v in range(variables)])
             edge = jnp.stack(
                 [
                     jnp.broadcast_to(edges[v, pl.ds(w + 6, 1), :], (BLOCKS, LANES))
@@ -188,7 +189,7 @@
         lax.fori_loop(0, rows + 4, make_images, 0, unroll=4)
 
         def interpolate(i, carry):
-            at = pl.multiple_of(i * BLOCKS, BLOCKS)
+            at = i * PITCH
             row_w = axis_weights(position[0, pl.ds(at, BLOCKS), :])
             col_w = axis_weights(position[1, pl.ds(at, BLOCKS), :])
             row_w = [jnp.concatenate([w] * variables, axis=0) for w in row_w]
@@ -208,7 +209,8 @@
                 line = row_n[r] * line
                 outer = line if outer is None else outer + line
             total = inner + outer.astype(jnp.float32)
-            interp[l, pl.ds(pl.multiple_of(i * pack, pack), pack), :] = total
+            for v in range(variables):
+                interp[l, v, pl.ds(at, BLOCKS), :] = total[v * BLOCKS : (v + 1) * BLOCKS]
             return carry
 
         lax.fori_loop(0, rows, interpolate, 0, unroll=4)
@@ -220,7 +222,7 @@
         for jb in range(BLOCKS):
             lanes = slice(jb * LANES, (jb + 1) * LANES)
             field = jnp.concatenate(
-                [interp[l, pl.ds(v * BLOCKS + jb, rows, stride=pack), :] for l in range(levels)],
+                [interp[l, v, pl.ds(jb, rows, stride=PITCH), :] for l in range(levels)],
                 axis=0,
             )
             column = jnp.dot(
@@ -295,12 +297,12 @@
         ],
         out_specs=pl.BlockSpec((variables, 1, slots, levels * rows), lambda b: (0, b, 0, 0)),
         scratch_shapes=[
-            pltpu.VMEM(((rows + 16) * pack, LANES), jnp.float32),
+            pltpu.VMEM((variables, (rows + 16) * PITCH + 8, LANES), jnp.float32),
             pltpu.VMEM((variables, rows + 16, LANES), jnp.float32),
             pltpu.VMEM((5, rows + 4, pack, LANES), jnp.bfloat16),
             pltpu.VMEM((3, rows + 4, pack, LANES), jnp.float32),
-            pltpu.VMEM((2, rows * BLOCKS, LANES), jnp.float32),
-            pltpu.VMEM((levels, rows * pack, LANES), jnp.float32),
+            pltpu.VMEM((2, rows * PITCH + 8, LANES), jnp.float32),
+            pltpu.VMEM((levels, variables, rows * PITCH + 8, LANES), jnp.float32),
             pltpu.VMEM((levels * rows, lon_dev), jnp.bfloat16),
         ],
         compiler_params=pltpu.CompilerParams(vmem_limit_bytes=48 * 1024 * 1024),
@@ -320,19 +322,20 @@
     waves = slot_wavenumber * (NTRUNC // m_window)
     basis = fourier_basis(lax.axis_index("lev") * lon_dev, lon_dev, waves).T
     partial = step_sums(upstream, departure, fractions, heating, mixing, basis)
-    partial = partial.reshape(var_dev, lat_dev // ROWS, 2 * m_window, levels, ROWS)
-    partial = partial.transpose(3, 0, 1, 4, 2).reshape(levels, var_dev, lat_dev, 2 * m_window)
-    sums = lax.psum_scatter(partial, "lev", scatter_dimension=0, tiled=True)
-    coefficients = (
-        (sums * (1.0 / math.sqrt(NLON)))
-        .astype(jnp.bfloat16)
-        .reshape(-1, var_dev, lat_dev, 2, m_window)
-    )
-    owned = lax.all_to_all(coefficients, "lat", split_axis=4, concat_axis=2, tiled=True)
+    sums = partial
+    peers = lax.axis_size("lev")
+    for hop in range(1, peers):
+        sums = sums + lax.ppermute(partial, "lev", [(i, (i + hop) % peers) for i in range(peers)])
+    steps = lat_dev // ROWS
+    coefficients = (sums * (1.0 / math.sqrt(NLON))).astype(jnp.bfloat16)
+    coefficients = coefficients.reshape(var_dev, steps, 2, m_window, levels * ROWS)
+    owned = lax.all_to_all(coefficients, "lat", split_axis=3, concat_axis=1, tiled=True)
+    slots, degrees = legendre.shape[0], legendre.shape[2]
+    owned = owned.reshape(var_dev, -1, 2, slots, levels, ROWS)
     return jnp.einsum(
-        "sin,lvirs->snrvl",
-        legendre,
-        lax.all_gather(owned, "lev", axis=0, tiled=True),
+        "sbin,vbrsli->snrvl",
+        legendre.reshape(slots, -1, ROWS, degrees),
+        owned,
         preferred_element_type=jnp.float32,
     )
 

time: 204 us -> 162 us (0.79)
  between operations: 13.6 us -> 0.21 us
  Pallas kernels: 126 us -> 113 us
  waiting for transfers between devices: 16.2 us -> 6.61 us
  local copies, waits for them, and re-layouts: 19.1 us -> 15.1 us
  blocking collectives: 15.1 us -> 11.6 us
  starting transfers between devices: 8.97 us -> 11.1 us
    reduce_scatter x1 -> x0, waiting for transfers between devices: 14.3 us -> none  [shards(): sums = lax.psum_scatter(partial, 'lev', scatter_dimension=0, tiled=True)]
    pallas_call x1, Pallas kernels: 126 us -> 113 us  [step_sums(): pl.pallas_call(column_kernel, grid=(steps,), out_shape=jax.ShapeDtypeStru...]
    all_gather x1 -> x0, blocking collectives: 4.94 us -> none  [shards(): lax.all_gather(owned, 'lev', axis=0, tiled=True)]
    ppermute x0 -> x1, waiting for transfers between devices: none -> 4.7 us  [shards(): lax.ppermute(partial, 'lev', [(i, (i + hop) % peers) for i in range(peers)])]
    reshape x4 -> x2, local copies, waits for them, and re-layouts: 4.15 us -> 0.34 us  [the longest x1 0.24 us: shards(): owned = owned.reshape(var_dev, -1, 2, slots, levels, ROWS)]
  transfers between devices with their start and end apart: 5 -> 5, of which waited for: 3 -> 3; matrix products, arithmetic and copies ran while one was open for 5% -> 6% of each run, Pallas kernels for 0% -> 0%
where the time goes in v2:
time: 162 us
  Pallas kernels  113 us (70%)
  local copies, waits for them, and re-layouts  15.1 us (9%)
  blocking collectives  11.6 us (7%)
  starting transfers between devices  11.1 us (7%)
  waiting for transfers between devices  6.61 us (4%)
  other arithmetic  3.67 us (2%)
    pallas_call x1, Pallas kernels, step_sums(): pl.pallas_call(column_kernel, grid=(steps,), out_shape=jax.ShapeDtypeStru...  113 us
    all_to_all x1, blocking collectives, shards(): lax.all_to_all(coefficients, 'lat', split_axis=3, concat_axis=1, tiled=True)  11.6 us
    ppermute x1, waiting for transfers between devices, shards(): lax.ppermute(partial, 'lev', [(i, (i + hop) % peers) for i in range(peers)])  4.7 us
    ppermute x1, starting transfers between devices, step_sums(): top = lax.ppermute(lower, 'lat', north).astype(jnp.float32)  4.62 us
    mul x4, local copies, waits for them, and re-layouts, step_sums(): mixing[:, :, None, :, None] * unit[None, None, :, None, :]  4.04 us
  transfers between devices with their start and end apart: 5, of which 3 were waited for; matrix products, arithmetic and copies ran while one was open for 6% of the time, Pallas kernels for 0%

profile of v2, /device:TPU:0, one launch (start us, length us, event | category | flops | bytes accessed | tf_op | source)
XLA Modules:
  0.0 161.7 jit_solution(16786695373958499571)
XLA Ops:
  0.0 3.0 %fusion.6 = (bf16[8,2,256,2]{3,2,1,0:T(8,128)(2,1)S(1)}, bf16[8,2,256,2]{3,2,1,0:T(8,128)(2,1)}) fusion(bf16[8,2,256,1024]{3,2,1,0:T(8,128)(2,1)} %following.1), kind=kLoop, calls=%fused_computation.26 | loop fusion | bytes 65536 | tf_op jit(solution)/shard_map/slice | solution.py:246
  3.0 1.6 copy.20
  4.6 3.1 %collective-permute-start.1 = (bf16[8,2,256,2]{2,0,3,1:T(8,128)(2,1)S(1)}, bf16[8,2,256,2]{2,0,3,1:T(8,128)(2,1)S(1)}, u32[]{:S(2)}, u32[]{:S(2)}) collective-permute-start(bf16[8,2,256,2]{2,0,3,1:T(8,128)(2,1)S(1)} %copy.20), channel_id=1, source_target_pairs={{0,2},{2,0},{1,3},{3,1},{4,6},{6,4},{5,7},{7,5},{8,10},{10,8},{9,1... | collective-permute-start | bytes 49160 | tf_op jit(solution)/shard_map/ppermute | solution.py:245
  7.7 0.4 copy.19
  8.2 1.8 %fusion.5 = (bf16[8,2,2,1024]{3,2,1,0:T(2,128)(2,1)}, bf16[8,2,2,1024]{3,2,1,0:T(2,128)(2,1)S(1)}) fusion(bf16[8,2,256,1024]{3,2,1,0:T(8,128)(2,1)} %following.1), kind=kLoop, calls=%fused_computation.25 | loop fusion | bytes 262144 | tf_op jit(solution)/shard_map/slice | solution.py:253
  9.9 0.5 broadcast_multiply_fusion
  10.5 0.6 iota_add_fusion
  11.1 0.3 mul.54
  11.5 1.5 mul.51
  13.0 2.1 %mul.52 = f32[2,256,256]{2,1,0:T(8,128)S(1)} reshape(f32[2,8,32,8,32]{4,3,2,1,0:T(8,128)} %mul.51) | data formatting | bytes 1048576 | tf_op jit(solution)/shard_map/mul | solution.py:259
  15.5 0.6 pad.23.clone
  16.1 1.2 copy.12
  17.3 1.4 copy.13
  18.7 2.0 %pad_maximum_fusion.e_main.e_prev.e_following = bf16[8,2,256,128]{3,2,1,0:T(8,128)(2,1)S(1)} fusion(bf16[8,2,256,2]{3,2,1,0:T(8,128)(2,1)} %copy.13, bf16[8,2,256,2]{3,2,1,0:T(8,128)(2,1)S(1)} %copy.12, bf16[128]{0:T(256)(128)(2,1)S(1)} %copy-done.6), kind=kLoop, calls=%fused_computation.1 | loop fusion | flops 3145728 | bytes 1081600 | tf_op jit(solution)/shard_map/concatenate | solution.py:248
  20.8 1.3 collective-permute-start.3
  22.2 4.6 %collective-permute-start.2 = (bf16[8,2,2,1152]{3,2,1,0:T(2,128)(2,1)S(1)}, bf16[8,2,2,1152]{3,2,1,0:T(2,128)(2,1)S(1)}, u32[]{:S(2)}, u32[]{:S(2)}) collective-permute-start(bf16[8,2,2,1152]{3,2,1,0:T(2,128)(2,1)S(1)} %pad_maximum_fusion.1), channel_id=1, source_target_pairs={{0,4},{4,8},{8,12},{1,5},{5,9},{9,13},{2,6},{6,10},{10,14},{3,7},{... | collective-permute-start | bytes 221192 | tf_op jit(solution)/shard_map/ppermute | solution.py:254
  26.8 0.3 collective-permute-done.3
  27.2 1.6 collective-permute-done.2
  28.9 112.9 %shard_map.73 = f32[2,8,16,256]{3,2,1,0:T(8,128)S(1)} custom-call(bf16[8,2,256,1024]{3,2,1,0:T(8,128)(2,1)} %following.1, bf16[8,2,256,1024]{3,2,1,0:T(8,128)(2,1)} %following.1, bf16[8,2,256,1024]{3,2,1,0:T(8,128)(2,1)} %following.1, bf16[8,2,256,128]{3,2,1,0:T(8,128)(2,1)S(1)} %pad_maximum_fusion.e_main.e_prev.e_following, ...), custom_call_target="tpu_custom_call" | custom-call | tf_op jit(solution)/shard_map/pallas_call | solution.py:283
  141.8 2.0 %collective-permute-start.4 = (f32[2,8,16,256]{3,2,1,0:T(8,128)S(1)}, f32[2,8,16,256]{3,2,1,0:T(8,128)S(1)}, u32[]{:S(2)}, u32[]{:S(2)}) collective-permute-start(f32[2,8,16,256]{3,2,1,0:T(8,128)S(1)} %shard_map.73), channel_id=1, source_target_pairs={{0,2},{2,0},{1,3},{3,1},{4,6},{6,4},{5,7},{7,5},{8,10},{10,8},{9,1... | collective-permute-start | bytes 786440 | tf_op jit(solution)/shard_map/ppermute | solution.py:328
  143.7 4.7 %collective-permute-done.4 = f32[2,8,16,256]{3,2,1,0:T(8,128)S(1)} collective-permute-done((f32[2,8,16,256]{3,2,1,0:T(8,128)S(1)}, f32[2,8,16,256]{3,2,1,0:T(8,128)S(1)}, u32[]{:S(2)}, u32[]{:S(2)}) %collective-permute-start.4) | collective-permute-done | bytes 262176 | tf_op jit(solution)/shard_map/ppermute | solution.py:328
  148.6 11.6 %all_to_all.15 = bf16[2,8,2,8,256]{4,2,1,0,3:T(2,128)(2,1)S(1)} all-to-all(bf16[2,8,2,8,256]{4,2,1,0,3:T(2,128)(2,1)S(1)} %copy.14), channel_id=1, replica_groups=mesh['grp'=2,'lat'=4,'lev'=2,'fld'=2] {'lat'}, dimensions={3} | all-to-all | bytes 262144 | tf_op jit(solution)/shard_map/all_to_all | solution.py:332
  160.4 0.6 convolution_bitcast_fusion
  161.0 0.7 copy.16
  (34 shorter events, 1.1 us)
Async XLA Ops:
  0.0 160.4 %copy-start = (bf16[2,1024,512]{2,1,0:T(8,128)(2,1)S(1)}, bf16[2,1024,512]{2,1,0:T(8,128)(2,1)}, u32[]{:S(2)}) copy-start(bf16[2,1024,512]{2,1,0:T(8,128)(2,1)} %param.13) | copy-start | bytes 6291460
  3.0 7.0 %copy-start.7 = (s32[8]{0:T(128)S(1)}, s32[8]{0:T(128)}, u32[]{:S(2)}) copy-start(s32[8]{0:T(128)} %param.12) | copy-start | bytes 100
  4.6 6.9 %copy-start.4 = (f32[2,8,8]{2,1,0:T(8,128)S(1)}, f32[2,8,8]{2,1,0:T(8,128)}, u32[]{:S(2)}) copy-start(f32[2,8,8]{2,1,0:T(8,128)} %param.11) | copy-start | bytes 1540
  4.6 12.7 %collective-permute-start.1 = (bf16[8,2,256,2]{2,0,3,1:T(8,128)(2,1)S(1)}, bf16[8,2,256,2]{2,0,3,1:T(8,128)(2,1)S(1)}, u32[]{:S(2)}, u32[]{:S(2)}) collective-permute-start(bf16[8,2,256,2]{2,0,3,1:T(8,128)(2,1)S(1)} %copy.20), channel_id=1, source_target_pairs={{0,2},{2,0},{1,3},{3,1},{4,6},{6,4},{5,7},{7,5},{8,10},{10,8},{9,1... | collective-permute-start | bytes 49160 | tf_op jit(solution)/shard_map/ppermute | solution.py:245
  8.1 8.0 %collective-permute-start = (bf16[8,2,256,2]{2,0,3,1:T(8,128)(2,1)S(1)}, bf16[8,2,256,2]{2,0,3,1:T(8,128)(2,1)}, u32[]{:S(2)}, u32[]{:S(2)}) collective-permute-start(bf16[8,2,256,2]{2,0,3,1:T(8,128)(2,1)S(1)} %copy.19), channel_id=1, source_target_pairs={{2,0},{0,2},{3,1},{1,3},{6,4},{4,6},{7,5},{5,7},{10,8},{8,10},{11,... | collective-permute-start | bytes 49160 | tf_op jit(solution)/shard_map/ppermute | solution.py:246
  11.4 3.7 %copy-start.3 = (s32[1024]{0:T(1024)S(1)}, s32[1024]{0:T(1024)}, u32[]{:S(2)}) copy-start(s32[1024]{0:T(1024)} %iota_add_fusion) | copy-start | bytes 12292
  11.5 3.7 %copy-start.5 = (s32[8]{0:T(128)S(1)}, s32[8]{0:T(128)}, u32[]{:S(2)}) copy-start(s32[8]{0:T(128)} %broadcast_multiply_fusion) | copy-start | bytes 100
  16.1 2.6 %copy-start.6 = (bf16[128]{0:T(256)(128)(2,1)S(1)}, bf16[128]{0:T(256)(128)(2,1)}, u32[]{:S(2)}) copy-start(bf16[128]{0:T(256)(128)(2,1)} %pad.23.clone) | copy-start | bytes 772
  18.7 2.0 %copy-start.2 = (bf16[8,2,2,1024]{3,2,1,0:T(2,128)(2,1)S(1)}, bf16[8,2,2,1024]{3,2,1,0:T(2,128)(2,1)}, u32[]{:S(2)}) copy-start(bf16[8,2,2,1024]{3,2,1,0:T(2,128)(2,1)} %get-tuple-element.5) | copy-start | bytes 196612
  18.7 10.1 %copy-start.1 = (bf16[2,256,1024]{2,1,0:T(8,128)(2,1)S(1)}, bf16[2,256,1024]{2,1,0:T(8,128)(2,1)}, u32[]{:S(2)}) copy-start(bf16[2,256,1024]{2,1,0:T(8,128)(2,1)} %heating.1) | copy-start | bytes 3145732
  20.8 6.3 %collective-permute-start.3 = (bf16[8,2,2,1152]{3,2,1,0:T(2,128)(2,1)S(1)}, bf16[8,2,2,1152]{3,2,1,0:T(2,128)(2,1)S(1)}, u32[]{:S(2)}, u32[]{:S(2)}) collective-permute-start(bf16[8,2,2,1152]{3,2,1,0:T(2,128)(2,1)S(1)} %pad_maximum_fusion.2), channel_id=1, source_target_pairs={{4,0},{8,4},{12,8},{5,1},{9,5},{13,9},{6,2},{10,6},{14,10},{7,3},{... | collective-permute-start | bytes 221192 | tf_op jit(solution)/shard_map/ppermute | solution.py:255
  22.2 6.6 %collective-permute-start.2 = (bf16[8,2,2,1152]{3,2,1,0:T(2,128)(2,1)S(1)}, bf16[8,2,2,1152]{3,2,1,0:T(2,128)(2,1)S(1)}, u32[]{:S(2)}, u32[]{:S(2)}) collective-permute-start(bf16[8,2,2,1152]{3,2,1,0:T(2,128)(2,1)S(1)} %pad_maximum_fusion.1), channel_id=1, source_target_pairs={{0,4},{4,8},{8,12},{1,5},{5,9},{9,13},{2,6},{6,10},{10,14},{3,7},{... | collective-permute-start | bytes 221192 | tf_op jit(solution)/shard_map/ppermute | solution.py:254
  141.8 6.7 %collective-permute-start.4 = (f32[2,8,16,256]{3,2,1,0:T(8,128)S(1)}, f32[2,8,16,256]{3,2,1,0:T(8,128)S(1)}, u32[]{:S(2)}, u32[]{:S(2)}) collective-permute-start(f32[2,8,16,256]{3,2,1,0:T(8,128)S(1)} %shard_map.73), channel_id=1, source_target_pairs={{0,2},{2,0},{1,3},{3,1},{4,6},{6,4},{5,7},{7,5},{8,10},{10,8},{9,1... | collective-permute-start | bytes 786440 | tf_op jit(solution)/shard_map/ppermute | solution.py:328
